TPU v7x, 32 devices: a whole 2x2x4 slice. The times are simulated.
32 devices in a mesh: wave: 2 (over y), tile: 16 (over z, x, core).
Axes of the slice: x: 2, y: 2, z: 4, core: 2. Of those that a mesh axis runs over, the one named last changes fastest.
Arguments:
- coefficients: bfloat16 [256, 256, 4096], P('tile', 'wave'), may hold values from -2.09375 to 2.09375
- profile_basis: bfloat16 [4096, 512], replicated, may hold values from -0.26367188 to 0.26367188
- point_spread: bfloat16 [17, 17], replicated, may hold values from 0.0009994507 to 0.0099487305
- observed: bfloat16 [512, 256, 256], P(None, 'tile', 'wave'), may hold values from -6 to 6
Outputs:
- coef_grad: bfloat16 [256, 256, 4096], P('tile', 'wave')
All inputs are finite; a program needn't handle non-finite values.
Results may differ from a plain program's by a relative error of at most 0.0058.
Values may be sent and summed in bfloat16 or wider, within the bound.
A program may use at most 192 MiB of HBM per device.

v0:
```python
import jax
import jax.numpy as jnp
from jax import lax
from jax.sharding import PartitionSpec as P


def padded_2(block, sides, width):
    for axis, dim in sides:
        count = lax.axis_size(axis)
        forward = [(i, i + 1) for i in range(count - 1)]
        backward = [(target, source) for source, target in forward]
        low = lax.ppermute(
            lax.slice_in_dim(block, block.shape[dim] - width, None, axis=dim), axis, forward
        )
        high = lax.ppermute(lax.slice_in_dim(block, 0, width, axis=dim), axis, backward)
        block = jnp.concatenate([low, block, high], axis=dim)
    return block


def tables(kernel, width_in, width_out):
    shifts = lax.broadcasted_iota(jnp.int32, (width_in, width_out), 0) - lax.broadcasted_iota(
        jnp.int32, (width_in, width_out), 1
    )
    kernel_f = kernel.astype(jnp.float32)
    summed = jnp.zeros((kernel.shape[0], width_in, width_out), jnp.float32)
    for column in range(kernel.shape[1]):
        summed = (
            summed
            + kernel_f[:, column][:, None, None] * (shifts == column).astype(jnp.float32)[None]
        )
    return summed.astype(jnp.bfloat16)


def convolve(padded, table, out_rows):
    summed = None
    for height in range(table.shape[0]):
        contrib = jnp.einsum(
            "prj,jc->prc",
            padded[:, height : height + out_rows, :],
            table[height],
            preferred_element_type=jnp.float32,
        )
        summed = contrib if height == 0 else summed + contrib
    return summed


def shards(coefficients, profile_basis, point_spread, observed):
    opacity = jnp.einsum(
        "rck,kl->lrc", coefficients, profile_basis, preferred_element_type=jnp.float32
    )
    spectra = jnp.exp(-opacity).astype(jnp.bfloat16)
    flipped = point_spread[::-1, ::-1]
    half_width = point_spread.shape[0] // 2
    strip_rows = coefficients.shape[0]
    block_cols = spectra.shape[2]
    forward_tab = tables(point_spread, block_cols + 2 * half_width, block_cols)
    adjoint_tab = tables(flipped, block_cols + 2 * half_width, block_cols)
    padded = padded_2(spectra, (("wave", 2), ("tile", 1)), half_width)
    blurred = convolve(padded, forward_tab, strip_rows)
    residual = (blurred - observed.astype(jnp.float32)).astype(jnp.bfloat16)
    padded_resid = padded_2(residual, (("wave", 2), ("tile", 1)), half_width)
    adjoint_field = convolve(padded_resid, adjoint_tab, strip_rows)
    tau_grad = (-spectra.astype(jnp.float32) * adjoint_field).astype(jnp.bfloat16)
    coef_grad = jnp.einsum(
        "lrc,kl->rck", tau_grad, profile_basis, preferred_element_type=jnp.float32
    )
    return coef_grad.astype(jnp.bfloat16)


def solution(mesh):
    placed = (P("tile", "wave", None), P(), P(), P(None, "tile", "wave"))
    return jax.shard_map(
        shards, mesh=mesh, in_specs=placed, out_specs=P("tile", "wave", None), check_vma=False
    )
```

profile of v0, /device:TPU:25, one launch (start us, length us, event | category | flops | bytes accessed | tf_op | source)
XLA Modules:
  0.0 234.2 jit_solution(15061565907038610768)
XLA Ops:
  0.0 13.6 %exponential_convert_fusion = bf16[512,16,128]{0,2,1:T(8,128)(2,1)S(1)} fusion(bf16[16,128,4096]{2,1,0:T(8,128)(2,1)} %param.4, bf16[4096,512]{1,0:T(8,128)(2,1)} %param.5), kind=kOutput, calls=%fused_computation.6 | convolution fusion | flops 8592031744 | bytes 23068672 | tf_op jit(solution)/shard_map/rck,kl->lrc/dot_general | solution.py:48
  13.6 3.2 %collective-permute-start = (bf16[512,16,8]{0,2,1:T(8,128)(2,1)S(1)}, bf16[512,16,8]{0,2,1:T(8,128)(2,1)S(1)}, u32[]{:S(2)}, u32[]{:S(2)}) collective-permute-start(bf16[512,16,8]{0,2,1:T(8,128)(2,1)S(1)} %get-tuple-element.45), channel_id=1, source_target_pairs={{0,16},{1,17},{2,18},{3,19},{4,20},{5,21},{6,22},{7,23},{8,24},{9,... | collective-permute-start | bytes 393224 | tf_op jit(solution)/shard_map/ppermute | solution.py:12
  18.7 4.4 %copy.6 = bf16[512,16,128]{0,2,1:T(8,128)(2,1)} copy(bf16[512,16,128]{2,1,0:T(8,128)(2,1)} %param.7) | data formatting | bytes 4194304 | tf_op args[3]
  23.9 3.3 %collective-permute-start.3 = (bf16[512,8,144]{0,2,1:T(8,128)(2,1)S(1)}, bf16[512,8,144]{0,2,1:T(8,128)(2,1)S(1)}, u32[]{:S(2)}, u32[]{:S(2)}) collective-permute-start(bf16[512,8,144]{0,2,1:T(8,128)(2,1)S(1)} %get-tuple-element.42), channel_id=1, source_target_pairs={{1,0},{2,1},{3,2},{4,3},{5,4},{6,5},{7,6},{8,7},{9,8},{10,9},{11,1... | collective-permute-start | bytes 3538952 | tf_op jit(solution)/shard_map/ppermute | solution.py:15
  29.0 3.3 %collective-permute-start.2 = (bf16[512,8,144]{0,2,1:T(8,128)(2,1)S(1)}, bf16[512,8,144]{0,2,1:T(8,128)(2,1)S(1)}, u32[]{:S(2)}, u32[]{:S(2)}) collective-permute-start(bf16[512,8,144]{0,2,1:T(8,128)(2,1)S(1)} %get-tuple-element.41), channel_id=1, source_target_pairs={{0,1},{1,2},{2,3},{3,4},{4,5},{5,6},{6,7},{7,8},{8,9},{9,10},{10,1... | collective-permute-start | bytes 3538952 | tf_op jit(solution)/shard_map/ppermute | solution.py:12
  34.2 20.6 %collective-permute-done.3 = bf16[512,8,144]{0,2,1:T(8,128)(2,1)S(1)} collective-permute-done((bf16[512,8,144]{0,2,1:T(8,128)(2,1)S(1)}, bf16[512,8,144]{0,2,1:T(8,128)(2,1)S(1)}, u32[]{:S(2)}, u32[]{:S(2)}) %collective-permute-start.3) | collective-permute-done | bytes 1179680 | tf_op jit(solution)/shard_map/ppermute | solution.py:15
  58.4 2.9 %fusion.61 = f32[512,16,128]{0,2,1:T(8,128)} fusion(bf16[17,144,128]{2,1,0:T(8,128)(2,1)S(1)} %add_convert_fusion.1, bf16[512,8,144]{0,2,1:T(8,128)(2,1)S(1)} %collective-permute-done.3, bf16[512,16,8]{0,2,1:T(8,128)(2,1)S(1)} %copy-done.21, bf16[512,16,128]{0,2,1:T(8,128)(2,1)S(1)} %exponential_convert_fusion, bf16[512,16,8]{0,2,1:T(8,128)(2,1)S(1)} %copy-done.19), kind=kOutput, calls=%fused_computation.93 | convolution fusion | flops 316145664 | bytes 7770112 | tf_op jit(solution)/shard_map/prj,jc->prc/dot_general | solution.py:37
  61.3 2.9 %fusion.60 = f32[512,16,128]{0,2,1:T(8,128)} fusion(bf16[17,144,128]{2,1,0:T(8,128)(2,1)S(1)} %add_convert_fusion.1, bf16[512,8,144]{0,2,1:T(8,128)(2,1)S(1)} %collective-permute-done.3, bf16[512,16,8]{0,2,1:T(8,128)(2,1)S(1)} %copy-done.21, bf16[512,16,128]{0,2,1:T(8,128)(2,1)S(1)} %exponential_convert_fusion, bf16[512,16,8]{0,2,1:T(8,128)(2,1)S(1)} %copy-done.19), kind=kOutput, calls=%fused_computation.91 | convolution fusion | flops 316145664 | bytes 7770112 | tf_op jit(solution)/shard_map/prj,jc->prc/dot_general | solution.py:37
  67.0 2.8 %fusion.58 = f32[512,16,128]{0,2,1:T(8,128)} fusion(bf16[17,144,128]{2,1,0:T(8,128)(2,1)S(1)} %add_convert_fusion.1, bf16[512,8,144]{0,2,1:T(8,128)(2,1)S(1)} %collective-permute-done.3, bf16[512,16,8]{0,2,1:T(8,128)(2,1)S(1)} %copy-done.21, bf16[512,16,128]{0,2,1:T(8,128)(2,1)S(1)} %exponential_convert_fusion, bf16[512,16,8]{0,2,1:T(8,128)(2,1)S(1)} %copy-done.19), kind=kOutput, calls=%fused_computation.87 | convolution fusion | flops 316145664 | bytes 7770112 | tf_op jit(solution)/shard_map/prj,jc->prc/dot_general | solution.py:37
  72.6 2.9 %fusion.72 = f32[512,16,128]{0,2,1:T(8,128)} fusion(bf16[17,144,128]{2,1,0:T(8,128)(2,1)S(1)} %add_convert_fusion.1, bf16[512,16,8]{0,2,1:T(8,128)(2,1)S(1)} %copy-done.21, bf16[512,16,128]{0,2,1:T(8,128)(2,1)S(1)} %exponential_convert_fusion, bf16[512,16,8]{0,2,1:T(8,128)(2,1)S(1)} %copy-done.19, bf16[512,8,144]{0,2,1:T(8,128)(2,1)S(1)} %collective-permute-done.2), kind=kOutput, calls=%fused_computation.115 | convolution fusion | flops 316145664 | bytes 7770112 | tf_op jit(solution)/shard_map/prj,jc->prc/dot_general | solution.py:37
  81.0 2.9 %fusion.69 = f32[512,16,128]{0,2,1:T(8,128)} fusion(bf16[17,144,128]{2,1,0:T(8,128)(2,1)S(1)} %add_convert_fusion.1, bf16[512,16,8]{0,2,1:T(8,128)(2,1)S(1)} %copy-done.21, bf16[512,16,128]{0,2,1:T(8,128)(2,1)S(1)} %exponential_convert_fusion, bf16[512,16,8]{0,2,1:T(8,128)(2,1)S(1)} %copy-done.19, bf16[512,8,144]{0,2,1:T(8,128)(2,1)S(1)} %collective-permute-done.2), kind=kOutput, calls=%fused_computation.109 | convolution fusion | flops 316145664 | bytes 7770112 | tf_op jit(solution)/shard_map/prj,jc->prc/dot_general | solution.py:37
  95.1 20.3 %subtract_convert_fusion = bf16[512,16,128]{0,2,1:T(8,128)(2,1)S(1)} fusion(bf16[512,16,128]{0,2,1:T(8,128)(2,1)S(1)} %copy-done.2, f32[512,16,128]{0,2,1:T(8,128)} %fusion.58, f32[512,16,128]{0,2,1:T(8,128)} %fusion.59, f32[512,16,128]{0,2,1:T(8,128)} %fusion.60, f32[512,16,128]{0,2,1:T(8,128)} %fusion.61, f32[512,16,128]{0,2,1:T(8,128)} %fusion.62, ...), kind=kOutput, calls=%fused_computation.5 | convolution fusion | flops 336068608 | bytes 74878976 | tf_op jit(solution)/shard_map/prj,jc->prc/dot_general | solution.py:37
  115.5 3.9 %collective-permute-start.4 = (bf16[512,16,8]{0,2,1:T(8,128)(2,1)S(1)}, bf16[512,16,8]{0,2,1:T(8,128)(2,1)S(1)}, u32[]{:S(2)}, u32[]{:S(2)}) collective-permute-start(bf16[512,16,8]{0,2,1:T(8,128)(2,1)S(1)} %get-tuple-element.43), channel_id=1, source_target_pairs={{0,16},{1,17},{2,18},{3,19},{4,20},{5,21},{6,22},{7,23},{8,24},{9,... | collective-permute-start | bytes 393224 | tf_op jit(solution)/shard_map/ppermute | solution.py:12
  121.3 3.8 %collective-permute-done.5 = bf16[512,16,8]{0,2,1:T(8,128)(2,1)S(1)} collective-permute-done((bf16[512,16,8]{0,2,1:T(8,128)(2,1)S(1)}, bf16[512,16,8]{0,2,1:T(8,128)(2,1)S(1)}, u32[]{:S(2)}, u32[]{:S(2)}) %collective-permute-start.5) | collective-permute-done | bytes 131104 | tf_op jit(solution)/shard_map/ppermute | solution.py:15
  129.4 2.9 %add_convert_fusion = bf16[17,144,128]{2,1,0:T(8,128)(2,1)S(1)} fusion(f32[17]{0:T(128)S(1)} %get-tuple-element.23, f32[17]{0:T(128)S(1)} %get-tuple-element.24, f32[17]{0:T(128)S(1)} %get-tuple-element.25, f32[17]{0:T(128)S(1)} %get-tuple-element.26, f32[17]{0:T(128)S(1)} %get-tuple-element.27, f32[17]{0:T(128)S(1)} %get-tuple-element.28, ...), kind=kLoop, calls=%fused_computation.14 | loop fusion | flops 10653696 | bytes 1881220 | tf_op jit(solution)/shard_map/convert_element_type | solution.py:31
  132.3 3.9 %collective-permute-start.6 = (bf16[512,8,144]{0,2,1:T(8,128)(2,1)}, bf16[512,8,144]{0,2,1:T(8,128)(2,1)S(1)}, u32[]{:S(2)}, u32[]{:S(2)}) collective-permute-start(bf16[512,8,144]{0,2,1:T(8,128)(2,1)} %get-tuple-element.39), channel_id=1, source_target_pairs={{0,1},{1,2},{2,3},{3,4},{4,5},{5,6},{6,7},{7,8},{8,9},{9,10},{10,1... | collective-permute-start | bytes 3538952 | tf_op jit(solution)/shard_map/ppermute | solution.py:12
  136.2 4.4 %fusion.48 = f32[512,16,128]{0,2,1:T(8,128)} fusion(bf16[17,144,128]{2,1,0:T(8,128)(2,1)S(1)} %add_convert_fusion, bf16[512,16,8]{0,2,1:T(8,128)(2,1)} %copy-done.24, bf16[512,16,128]{0,2,1:T(8,128)(2,1)} %copy-done, bf16[512,16,8]{0,2,1:T(8,128)(2,1)} %copy-done.22), kind=kOutput, calls=%fused_computation.67 | convolution fusion | flops 309067776 | bytes 6590464 | tf_op jit(solution)/shard_map/prj,jc->prc/dot_general | solution.py:37
  140.6 16.6 %collective-permute-done.7 = bf16[512,8,144]{0,2,1:T(8,128)(2,1)S(1)} collective-permute-done((bf16[512,8,144]{0,2,1:T(8,128)(2,1)}, bf16[512,8,144]{0,2,1:T(8,128)(2,1)S(1)}, u32[]{:S(2)}, u32[]{:S(2)}) %collective-permute-start.7) | collective-permute-done | bytes 1179680 | tf_op jit(solution)/shard_map/ppermute | solution.py:15
  157.3 2.8 %fusion.46 = f32[512,16,128]{0,2,1:T(8,128)} fusion(bf16[17,144,128]{2,1,0:T(8,128)(2,1)S(1)} %add_convert_fusion, bf16[512,8,144]{0,2,1:T(8,128)(2,1)S(1)} %collective-permute-done.7, bf16[512,16,8]{0,2,1:T(8,128)(2,1)S(1)} %copy-done.25, bf16[512,16,128]{0,2,1:T(8,128)(2,1)S(1)} %copy-done.1, bf16[512,16,8]{0,2,1:T(8,128)(2,1)S(1)} %copy-done.23), kind=kOutput, calls=%fused_computation.63 | convolution fusion | flops 316145664 | bytes 7770112 | tf_op jit(solution)/shard_map/prj,jc->prc/dot_general | solution.py:37
  165.7 2.9 %fusion.43 = f32[512,16,128]{0,2,1:T(8,128)} fusion(bf16[17,144,128]{2,1,0:T(8,128)(2,1)S(1)} %add_convert_fusion, bf16[512,8,144]{0,2,1:T(8,128)(2,1)S(1)} %collective-permute-done.7, bf16[512,16,8]{0,2,1:T(8,128)(2,1)S(1)} %copy-done.25, bf16[512,16,128]{0,2,1:T(8,128)(2,1)S(1)} %copy-done.1, bf16[512,16,8]{0,2,1:T(8,128)(2,1)S(1)} %copy-done.23), kind=kOutput, calls=%fused_computation.57 | convolution fusion | flops 316145664 | bytes 7770112 | tf_op jit(solution)/shard_map/prj,jc->prc/dot_general | solution.py:37
  168.6 2.9 %fusion.42 = f32[512,16,128]{0,2,1:T(8,128)} fusion(bf16[17,144,128]{2,1,0:T(8,128)(2,1)S(1)} %add_convert_fusion, bf16[512,8,144]{0,2,1:T(8,128)(2,1)S(1)} %collective-permute-done.7, bf16[512,16,8]{0,2,1:T(8,128)(2,1)S(1)} %copy-done.25, bf16[512,16,128]{0,2,1:T(8,128)(2,1)S(1)} %copy-done.1, bf16[512,16,8]{0,2,1:T(8,128)(2,1)S(1)} %copy-done.23), kind=kOutput, calls=%fused_computation.55 | convolution fusion | flops 316145664 | bytes 7770112 | tf_op jit(solution)/shard_map/prj,jc->prc/dot_general | solution.py:37
  182.7 2.8 %fusion.53 = f32[512,16,128]{0,2,1:T(8,128)} fusion(bf16[17,144,128]{2,1,0:T(8,128)(2,1)S(1)} %add_convert_fusion, bf16[512,16,8]{0,2,1:T(8,128)(2,1)S(1)} %copy-done.25, bf16[512,16,128]{0,2,1:T(8,128)(2,1)S(1)} %copy-done.1, bf16[512,16,8]{0,2,1:T(8,128)(2,1)S(1)} %copy-done.23, bf16[512,8,144]{0,2,1:T(8,128)(2,1)S(1)} %collective-permute-done.6), kind=kOutput, calls=%fused_computation.77 | convolution fusion | flops 316145664 | bytes 7770112 | tf_op jit(solution)/shard_map/prj,jc->prc/dot_general | solution.py:37
  193.8 2.9 %fusion.49 = f32[512,16,128]{0,2,1:T(8,128)} fusion(bf16[17,144,128]{2,1,0:T(8,128)(2,1)S(1)} %add_convert_fusion, bf16[512,16,8]{0,2,1:T(8,128)(2,1)S(1)} %copy-done.25, bf16[512,16,128]{0,2,1:T(8,128)(2,1)S(1)} %copy-done.1, bf16[512,16,8]{0,2,1:T(8,128)(2,1)S(1)} %copy-done.23, bf16[512,8,144]{0,2,1:T(8,128)(2,1)S(1)} %collective-permute-done.6), kind=kOutput, calls=%fused_computation.69 | convolution fusion | flops 316145664 | bytes 7770112 | tf_op jit(solution)/shard_map/prj,jc->prc/dot_general | solution.py:37
  199.5 34.5 %convolution_convert_fusion = bf16[16,128,4096]{2,1,0:T(8,128)(2,1)} fusion(bf16[4096,512]{1,0:T(8,128)(2,1)} %param.5, f32[512,16,128]{0,2,1:T(8,128)} %fusion.41, f32[512,16,128]{0,2,1:T(8,128)} %fusion.42, f32[512,16,128]{0,2,1:T(8,128)} %fusion.43, f32[512,16,128]{0,2,1:T(8,128)} %fusion.44, f32[512,16,128]{0,2,1:T(8,128)} %fusion.45, ...), kind=kOutput, calls=%fused_computation | convolution fusion | flops 8935440384 | bytes 93753344 | tf_op jit(solution)/shard_map/lrc,kl->rck/dot_general | solution.py:64
  (104 shorter events, 66.2 us)
Async XLA Ops:
  0.0 18.2 %copy-start.26 = (bf16[17,17]{1,0:T(8,128)(2,1)S(1)}, bf16[17,17]{1,0:T(8,128)(2,1)}, u32[]{:S(2)}) copy-start(bf16[17,17]{1,0:T(8,128)(2,1)} %param.6) | copy-start | bytes 1738
  13.6 9.5 %collective-permute-start = (bf16[512,16,8]{0,2,1:T(8,128)(2,1)S(1)}, bf16[512,16,8]{0,2,1:T(8,128)(2,1)S(1)}, u32[]{:S(2)}, u32[]{:S(2)}) collective-permute-start(bf16[512,16,8]{0,2,1:T(8,128)(2,1)S(1)} %get-tuple-element.45), channel_id=1, source_target_pairs={{0,16},{1,17},{2,18},{3,19},{4,20},{5,21},{6,22},{7,23},{8,24},{9,... | collective-permute-start | bytes 393224 | tf_op jit(solution)/shard_map/ppermute | solution.py:12
  16.8 6.4 %collective-permute-start.1 = (bf16[512,16,8]{0,2,1:T(8,128)(2,1)S(1)}, bf16[512,16,8]{0,2,1:T(8,128)(2,1)S(1)}, u32[]{:S(2)}, u32[]{:S(2)}) collective-permute-start(bf16[512,16,8]{0,2,1:T(8,128)(2,1)S(1)} %get-tuple-element.46), channel_id=1, source_target_pairs={{16,0},{17,1},{18,2},{19,3},{20,4},{21,5},{22,6},{23,7},{24,8},{25... | collective-permute-start | bytes 393224 | tf_op jit(solution)/shard_map/ppermute | solution.py:15
  18.2 9.2 %copy-start.4 = (f32[144,128]{1,0:T(8,128)}, f32[144,128]{1,0:T(8,128)S(1)}, u32[]{:S(2)}) copy-start(f32[144,128]{1,0:T(8,128)S(1)} %get-tuple-element.60) | copy-start | bytes 221188
  18.2 9.2 %copy-start.5 = (f32[144,128]{1,0:T(8,128)}, f32[144,128]{1,0:T(8,128)S(1)}, u32[]{:S(2)}) copy-start(f32[144,128]{1,0:T(8,128)S(1)} %get-tuple-element.57) | copy-start | bytes 221188
  18.2 9.2 %copy-start.6 = (f32[144,128]{1,0:T(8,128)}, f32[144,128]{1,0:T(8,128)S(1)}, u32[]{:S(2)}) copy-start(f32[144,128]{1,0:T(8,128)S(1)} %get-tuple-element.58) | copy-start | bytes 221188
  18.2 9.1 %copy-start.7 = (f32[144,128]{1,0:T(8,128)}, f32[144,128]{1,0:T(8,128)S(1)}, u32[]{:S(2)}) copy-start(f32[144,128]{1,0:T(8,128)S(1)} %get-tuple-element.55) | copy-start | bytes 221188
  18.3 9.1 %copy-start.8 = (f32[144,128]{1,0:T(8,128)}, f32[144,128]{1,0:T(8,128)S(1)}, u32[]{:S(2)}) copy-start(f32[144,128]{1,0:T(8,128)S(1)} %get-tuple-element.56) | copy-start | bytes 221188
  23.9 30.9 %collective-permute-start.3 = (bf16[512,8,144]{0,2,1:T(8,128)(2,1)S(1)}, bf16[512,8,144]{0,2,1:T(8,128)(2,1)S(1)}, u32[]{:S(2)}, u32[]{:S(2)}) collective-permute-start(bf16[512,8,144]{0,2,1:T(8,128)(2,1)S(1)} %get-tuple-element.42), channel_id=1, source_target_pairs={{1,0},{2,1},{3,2},{4,3},{5,4},{6,5},{7,6},{8,7},{9,8},{10,9},{11,1... | collective-permute-start | bytes 3538952 | tf_op jit(solution)/shard_map/ppermute | solution.py:15
  27.2 7.0 %copy-start.11 = (f32[144,128]{1,0:T(8,128)}, f32[144,128]{1,0:T(8,128)S(1)}, u32[]{:S(2)}) copy-start(f32[144,128]{1,0:T(8,128)S(1)} %fusion.40) | copy-start | bytes 221188
  27.2 6.9 %copy-start.12 = (f32[144,128]{1,0:T(8,128)}, f32[144,128]{1,0:T(8,128)S(1)}, u32[]{:S(2)}) copy-start(f32[144,128]{1,0:T(8,128)S(1)} %get-tuple-element.51) | copy-start | bytes 221188
  27.2 6.9 %copy-start.13 = (f32[144,128]{1,0:T(8,128)}, f32[144,128]{1,0:T(8,128)S(1)}, u32[]{:S(2)}) copy-start(f32[144,128]{1,0:T(8,128)S(1)} %get-tuple-element.52) | copy-start | bytes 221188
  29.0 25.8 %copy-start.19 = (bf16[512,16,8]{0,2,1:T(8,128)(2,1)S(1)}, bf16[512,16,8]{0,2,1:T(8,128)(2,1)}, u32[]{:S(2)}) copy-start(bf16[512,16,8]{0,2,1:T(8,128)(2,1)} %copy-done.18) | copy-start | bytes 393220
  29.0 25.8 %copy-start.21 = (bf16[512,16,8]{0,2,1:T(8,128)(2,1)S(1)}, bf16[512,16,8]{0,2,1:T(8,128)(2,1)}, u32[]{:S(2)}) copy-start(bf16[512,16,8]{0,2,1:T(8,128)(2,1)} %copy-done.20) | copy-start | bytes 393220
  29.0 43.6 %collective-permute-start.2 = (bf16[512,8,144]{0,2,1:T(8,128)(2,1)S(1)}, bf16[512,8,144]{0,2,1:T(8,128)(2,1)S(1)}, u32[]{:S(2)}, u32[]{:S(2)}) collective-permute-start(bf16[512,8,144]{0,2,1:T(8,128)(2,1)S(1)} %get-tuple-element.41), channel_id=1, source_target_pairs={{0,1},{1,2},{2,3},{3,4},{4,5},{5,6},{6,7},{7,8},{8,9},{9,10},{10,1... | collective-permute-start | bytes 3538952 | tf_op jit(solution)/shard_map/ppermute | solution.py:12
  115.4 11.4 %copy-start = (bf16[512,16,128]{0,2,1:T(8,128)(2,1)}, bf16[512,16,128]{0,2,1:T(8,128)(2,1)S(1)}, u32[]{:S(2)}) copy-start(bf16[512,16,128]{0,2,1:T(8,128)(2,1)S(1)} %subtract_convert_fusion) | copy-start | bytes 6291460
  115.5 5.8 %collective-permute-start.4 = (bf16[512,16,8]{0,2,1:T(8,128)(2,1)S(1)}, bf16[512,16,8]{0,2,1:T(8,128)(2,1)S(1)}, u32[]{:S(2)}, u32[]{:S(2)}) collective-permute-start(bf16[512,16,8]{0,2,1:T(8,128)(2,1)S(1)} %get-tuple-element.43), channel_id=1, source_target_pairs={{0,16},{1,17},{2,18},{3,19},{4,20},{5,21},{6,22},{7,23},{8,24},{9,... | collective-permute-start | bytes 393224 | tf_op jit(solution)/shard_map/ppermute | solution.py:12
  119.4 5.7 %collective-permute-start.5 = (bf16[512,16,8]{0,2,1:T(8,128)(2,1)S(1)}, bf16[512,16,8]{0,2,1:T(8,128)(2,1)S(1)}, u32[]{:S(2)}, u32[]{:S(2)}) collective-permute-start(bf16[512,16,8]{0,2,1:T(8,128)(2,1)S(1)} %get-tuple-element.44), channel_id=1, source_target_pairs={{16,0},{17,1},{18,2},{19,3},{20,4},{21,5},{22,6},{23,7},{24,8},{25... | collective-permute-start | bytes 393224 | tf_op jit(solution)/shard_map/ppermute | solution.py:15
  126.9 30.4 %collective-permute-start.7 = (bf16[512,8,144]{0,2,1:T(8,128)(2,1)}, bf16[512,8,144]{0,2,1:T(8,128)(2,1)S(1)}, u32[]{:S(2)}, u32[]{:S(2)}) collective-permute-start(bf16[512,8,144]{0,2,1:T(8,128)(2,1)} %get-tuple-element.40), channel_id=1, source_target_pairs={{1,0},{2,1},{3,2},{4,3},{5,4},{6,5},{7,6},{8,7},{9,8},{10,9},{11,1... | collective-permute-start | bytes 3538952 | tf_op jit(solution)/shard_map/ppermute | solution.py:15
  132.3 64.5 %copy-start.3 = (bf16[17,144,128]{2,1,0:T(8,128)(2,1)}, bf16[17,144,128]{2,1,0:T(8,128)(2,1)S(1)}, u32[]{:S(2)}) copy-start(bf16[17,144,128]{2,1,0:T(8,128)(2,1)S(1)} %add_convert_fusion) | copy-start | bytes 1880068
  132.3 25.0 %copy-start.1 = (bf16[512,16,128]{0,2,1:T(8,128)(2,1)S(1)}, bf16[512,16,128]{0,2,1:T(8,128)(2,1)}, u32[]{:S(2)}) copy-start(bf16[512,16,128]{0,2,1:T(8,128)(2,1)} %copy-done) | copy-start | bytes 6291460
  132.3 25.0 %copy-start.23 = (bf16[512,16,8]{0,2,1:T(8,128)(2,1)S(1)}, bf16[512,16,8]{0,2,1:T(8,128)(2,1)}, u32[]{:S(2)}) copy-start(bf16[512,16,8]{0,2,1:T(8,128)(2,1)} %copy-done.22) | copy-start | bytes 393220
  132.3 25.0 %copy-start.25 = (bf16[512,16,8]{0,2,1:T(8,128)(2,1)S(1)}, bf16[512,16,8]{0,2,1:T(8,128)(2,1)}, u32[]{:S(2)}) copy-start(bf16[512,16,8]{0,2,1:T(8,128)(2,1)} %copy-done.24) | copy-start | bytes 393220
  132.3 44.8 %collective-permute-start.6 = (bf16[512,8,144]{0,2,1:T(8,128)(2,1)}, bf16[512,8,144]{0,2,1:T(8,128)(2,1)S(1)}, u32[]{:S(2)}, u32[]{:S(2)}) collective-permute-start(bf16[512,8,144]{0,2,1:T(8,128)(2,1)} %get-tuple-element.39), channel_id=1, source_target_pairs={{0,1},{1,2},{2,3},{3,4},{4,5},{5,6},{6,7},{7,8},{8,9},{9,10},{10,1... | collective-permute-start | bytes 3538952 | tf_op jit(solution)/shard_map/ppermute | solution.py:12
  (11 other events, 47.7 us)
where the time goes:
time: 235 us; the launch traced here: 234 us
  matrix products  157 us (67%)
  waiting for transfers between devices  41.6 us (18%)
  starting transfers between devices  22 us (9%)
  local copies, waits for them, and re-layouts  7.67 us (3%)
  other arithmetic  5 us (2%)
    dot_general x33, matrix products, convolve(): jnp.einsum('prj,jc->prc', padded[:, height:height + out_rows, :], table[h...  109 us
    ppermute x4, waiting for transfers between devices, padded_2(): lax.ppermute(lax.slice_in_dim(block, 0, width, axis=dim), axis, backward)  41 us
    dot_general x1, matrix products, shards(): jnp.einsum('lrc,kl->rck', tau_grad, profile_basis, preferred_element_type...  34.5 us
    ppermute x4, starting transfers between devices, padded_2(): lax.ppermute(lax.slice_in_dim(block, block.shape[dim] - width, None, axis...  14.3 us
    dot_general x1, matrix products, shards(): jnp.einsum('rck,kl->lrc', coefficients, profile_basis, preferred_element_...  13.6 us
    ppermute x4, starting transfers between devices, padded_2(): lax.ppermute(lax.slice_in_dim(block, 0, width, axis=dim), axis, backward)  7.76 us
    unnamed x55, local copies, waits for them, and re-layouts  4.86 us
  transfers between devices with their start and end apart: 8, of which 4 were waited for; matrix products, arithmetic and copies ran while one was open for 23% of the time, Pallas kernels for 0%

commit v1 on v0

v1 whole, which is shorter than its diff:
```python
import functools

import jax
import jax.numpy as jnp
from jax import lax
from jax.experimental import pallas as pl
from jax.experimental.pallas import tpu as pltpu
from jax.sharding import PartitionSpec as P

MESH = pl.DeviceIdType.MESH
EDGE = 16
PATCH = 16
CHUNKS = 2
TILE_ROWS = 2
COL_RIGHT, COL_LEFT, ROW_UP, ROW_DOWN, UP_LEFT, UP_RIGHT, DOWN_LEFT, DOWN_RIGHT = range(8)


def stencil_matrix(psf_ref, out_ref, half, adjoint):
    width_in = PATCH + 2 * EDGE
    rows_in = PATCH + 2 * half
    total = rows_in * width_in
    psf = psf_ref[...]
    taps = 2 * half + 1
    lane = lax.broadcasted_iota(jnp.int32, (psf.shape[0], total), 1)
    height = jnp.zeros_like(lane)
    for m in range(1, rows_in):
        height = height + jnp.where(lane >= m * width_in, 1, 0)
    tap = lax.broadcasted_iota(jnp.int32, (psf.shape[0], total), 0)
    wanted = (taps - 1) - tap if adjoint else tap
    onehot = jnp.where(wanted == height, 1.0, 0.0).astype(jnp.bfloat16)
    spread = lax.dot_general(
        psf, onehot, (((0,), (0,)), ((), ())), preferred_element_type=jnp.float32
    )
    lane = lax.broadcasted_iota(jnp.int32, (PATCH, total), 1)
    height = jnp.zeros_like(lane)
    for m in range(1, rows_in):
        height = height + jnp.where(lane >= m * width_in, 1, 0)
    shift = (lane - height * width_in - (EDGE - half)
             - lax.broadcasted_iota(jnp.int32, (PATCH, total), 0))
    base = jnp.zeros((PATCH, total), jnp.float32)
    for b in range(taps):
        at = taps - 1 - b if adjoint else b
        base = base + jnp.where(shift == at, spread[b:b + 1, :], 0.0)
    for r in range(PATCH):
        rolled = base if r == 0 else pltpu.roll(base, r * width_in, 1)
        out_ref[r * PATCH:(r + 1) * PATCH, :] = rolled.astype(jnp.bfloat16)


def kernel(half, n_tile, n_wave, coef_ref, basis_hbm, psf_ref, obs_hbm, tau_ref,
           coef, basis, obs, spec, resid, fwd, adj,
           coef_sem, load_sem, send_sem, recv_sem):
    rows = spec.shape[0] - 2 * half
    cols = spec.shape[1] - 2 * EDGE
    waves = spec.shape[2]
    width = waves // CHUNKS
    tile = lax.axis_index("tile")
    wave = lax.axis_index("wave")
    has = {
        "up": tile > 0, "down": tile < n_tile - 1,
        "left": wave > 0, "right": wave < n_wave - 1,
    }
    device = {
        "up": {"tile": tile - 1}, "down": {"tile": tile + 1},
        "left": {"wave": wave - 1}, "right": {"wave": wave + 1},
    }
    odd = lax.rem(tile, 2)
    steps = rows // TILE_ROWS
    per_half = steps // 2

    def tile_at(t):
        return lax.rem(t + odd * per_half, steps)

    def coef_copy(t):
        at = tile_at(t) * TILE_ROWS
        return pltpu.make_async_copy(
            coef_ref.at[pl.ds(at, TILE_ROWS)], coef.at[pl.ds(at, TILE_ROWS)], coef_sem.at[t]
        )

    basis_copy = pltpu.make_async_copy(basis_hbm, basis, load_sem.at[0])
    obs_copy = pltpu.make_async_copy(obs_hbm, obs, load_sem.at[1])
    basis_copy.start()
    for t in range(steps):
        coef_copy(t).start()
    obs_copy.start()

    barrier = pltpu.get_barrier_semaphore()
    for side in has:
        @pl.when(has[side])
        def _(side=side):
            pl.semaphore_signal(barrier, inc=1, device_id=device[side], device_id_type=MESH)

    for field in (spec, resid):
        @pl.when(jnp.logical_not(has["up"]))
        def _(field=field):
            field[0:half] = jnp.zeros((half,) + field.shape[1:], field.dtype)

        @pl.when(jnp.logical_not(has["down"]))
        def _(field=field):
            field[half + rows:] = jnp.zeros((half,) + field.shape[1:], field.dtype)

        @pl.when(jnp.logical_not(has["left"]))
        def _(field=field):
            field[half:half + rows, 0:EDGE] = jnp.zeros((rows, EDGE, waves), field.dtype)

        @pl.when(jnp.logical_not(has["right"]))
        def _(field=field):
            field[half:half + rows, EDGE + cols:] = jnp.zeros((rows, EDGE, waves), field.dtype)

    peers = jnp.int32(0)
    for side in has:
        peers = peers + jnp.where(has[side], 1, 0)
    pl.semaphore_wait(barrier, peers)

    top, low = half, rows
    near = rows + half

    places = {
        COL_RIGHT: ("right", "left", (half, rows), cols, 0),
        COL_LEFT: ("left", "right", (half, rows), EDGE, EDGE + cols),
        ROW_UP: ("up", "down", (top, near), EDGE, EDGE),
        ROW_DOWN: ("down", "up", (low, 0), EDGE, EDGE),
        UP_LEFT: ("up", "down", (top, near), 0, 0),
        UP_RIGHT: ("up", "down", (top, near), EDGE + cols, EDGE + cols),
        DOWN_LEFT: ("down", "up", (low, 0), 0, 0),
        DOWN_RIGHT: ("down", "up", (low, 0), EDGE + cols, EDGE + cols),
    }

    def copy(which, chunk, kind):
        field = (spec, resid)[which]
        side, _, span, source, target = places[kind]
        lanes = pl.ds(chunk * width, width)
        if kind in (COL_RIGHT, COL_LEFT):
            src = field.at[pl.ds(half, rows), pl.ds(source, EDGE), lanes]
            dst = field.at[pl.ds(half, rows), pl.ds(target, EDGE), lanes]
        else:
            size = cols if kind in (ROW_UP, ROW_DOWN) else EDGE
            src = field.at[pl.ds(span[0], half), pl.ds(source, size), lanes]
            dst = field.at[pl.ds(span[1], half), pl.ds(target, size), lanes]
        return pltpu.make_async_remote_copy(
            src_ref=src, dst_ref=dst,
            send_sem=send_sem.at[which, chunk, kind],
            recv_sem=recv_sem.at[which, chunk, kind],
            device_id=device[side], device_id_type=MESH,
        )

    def start(which, chunk, kinds):
        for kind in kinds:
            @pl.when(has[places[kind][0]])
            def _(kind=kind):
                copy(which, chunk, kind).start()

    def arrive(which, chunk, kinds):
        for kind in kinds:
            @pl.when(has[places[kind][1]])
            def _(kind=kind):
                copy(which, chunk, kind).wait_recv()

    corners = (UP_LEFT, UP_RIGHT, DOWN_LEFT, DOWN_RIGHT)

    basis_copy.wait()
    for part in range(2):
        for chunk in range(CHUNKS):
            lanes = pl.ds(chunk * width, width)
            for s in range(per_half):
                if chunk == 0:
                    coef_copy(part * per_half + s).wait()

            @pl.loop(0, per_half)
            def _(s, part=part, lanes=lanes):
                at = tile_at(part * per_half + s) * TILE_ROWS
                block = coef[pl.ds(at, TILE_ROWS)].reshape(TILE_ROWS * cols, coef.shape[2])
                opacity = jnp.dot(block, basis[:, lanes], preferred_element_type=jnp.float32)
                spec[pl.ds(half + at, TILE_ROWS), EDGE:EDGE + cols, lanes] = (
                    jnp.exp(-opacity).astype(jnp.bfloat16).reshape(TILE_ROWS, cols, width)
                )

            upper = odd if part == 1 else 1 - odd

            @pl.when(jnp.logical_and(upper == 1, has["up"]))
            def _(chunk=chunk):
                copy(0, chunk, ROW_UP).start()

            @pl.when(jnp.logical_and(upper == 0, has["down"]))
            def _(chunk=chunk):
                copy(0, chunk, ROW_DOWN).start()

            if part == 1:
                start(0, chunk, (COL_RIGHT, COL_LEFT))

    stencil_matrix(psf_ref, fwd, half, False)
    stencil_matrix(psf_ref, adj, half, True)
    for chunk in range(CHUNKS):
        arrive(0, chunk, (COL_RIGHT, COL_LEFT))
        start(0, chunk, corners)
    obs_copy.wait()

    def window(field, i, lanes):
        patch = field[:, pl.ds(i * PATCH, PATCH + 2 * EDGE), lanes]
        return patch.reshape(patch.shape[0] * patch.shape[1], width)

    for chunk in range(CHUNKS):
        lanes = pl.ds(chunk * width, width)
        arrive(0, chunk, (ROW_UP, ROW_DOWN) + corners)

        @pl.loop(0, cols // PATCH)
        def _(i, lanes=lanes):
            blurred = jnp.dot(fwd[...], window(spec, i, lanes), preferred_element_type=jnp.float32)
            seen = obs[:, pl.ds(i * PATCH, PATCH), lanes].astype(jnp.float32)
            resid[half:half + rows, pl.ds(EDGE + i * PATCH, PATCH), lanes] = (
                blurred.reshape(rows, PATCH, width) - seen
            ).astype(jnp.bfloat16)

        start(1, chunk, (COL_RIGHT, COL_LEFT, ROW_UP, ROW_DOWN))
        arrive(1, chunk, (COL_RIGHT, COL_LEFT))
        start(1, chunk, corners)

    for chunk in range(CHUNKS):
        lanes = pl.ds(chunk * width, width)
        arrive(1, chunk, (ROW_UP, ROW_DOWN) + corners)

        @pl.loop(0, cols // PATCH)
        def _(i, lanes=lanes):
            field = jnp.dot(adj[...], window(resid, i, lanes), preferred_element_type=jnp.float32)
            own = spec[half:half + rows, pl.ds(EDGE + i * PATCH, PATCH), lanes].astype(jnp.float32)
            tau_ref[:, pl.ds(i * PATCH, PATCH), lanes] = (
                -own * field.reshape(rows, PATCH, width)
            ).astype(jnp.bfloat16)

    for which in range(2):
        for chunk in range(CHUNKS):
            for kind in places:
                @pl.when(has[places[kind][0]])
                def _(which=which, chunk=chunk, kind=kind):
                    copy(which, chunk, kind).wait_send()


def shards(n_tile, n_wave, coefficients, profile_basis, point_spread, observed):
    rows, cols, profiles = coefficients.shape
    waves = profile_basis.shape[1]
    half = point_spread.shape[0] // 2
    psf = jnp.pad(point_spread, ((0, 32 - point_spread.shape[0]), (0, 128 - point_spread.shape[1])))
    seen = observed.transpose(1, 2, 0)
    padded = (rows + 2 * half, cols + 2 * EDGE, waves)
    table = (PATCH * PATCH, (PATCH + 2 * half) * (PATCH + 2 * EDGE))
    vmem = pl.BlockSpec(memory_space=pltpu.VMEM)
    hbm = pl.BlockSpec(memory_space=pl.ANY)
    tau = pl.pallas_call(
        functools.partial(kernel, half, n_tile, n_wave),
        out_shape=jax.ShapeDtypeStruct((rows, cols, waves), jnp.bfloat16),
        in_specs=[hbm, hbm, vmem, hbm],
        out_specs=vmem,
        scratch_shapes=[
            pltpu.VMEM(coefficients.shape, jnp.bfloat16),
            pltpu.VMEM(profile_basis.shape, jnp.bfloat16),
            pltpu.VMEM(seen.shape, jnp.bfloat16),
            pltpu.VMEM(padded, jnp.bfloat16),
            pltpu.VMEM(padded, jnp.bfloat16),
            pltpu.VMEM(table, jnp.bfloat16),
            pltpu.VMEM(table, jnp.bfloat16),
            pltpu.SemaphoreType.DMA((rows // TILE_ROWS,)),
            pltpu.SemaphoreType.DMA((2,)),
            pltpu.SemaphoreType.DMA((2, CHUNKS, 8)),
            pltpu.SemaphoreType.DMA((2, CHUNKS, 8)),
        ],
        compiler_params=pltpu.CompilerParams(
            collective_id=0, has_side_effects=True, vmem_limit_bytes=56 * 1024 * 1024
        ),
    )(coefficients, profile_basis, psf, seen)
    grad = jnp.dot(
        tau.reshape(rows * cols, waves), profile_basis.T, preferred_element_type=jnp.float32
    )
    return grad.astype(jnp.bfloat16).reshape(rows, cols, profiles)


def solution(mesh):
    placed = (P("tile", "wave", None), P(), P(), P(None, "tile", "wave"))
    return jax.shard_map(
        functools.partial(shards, mesh.shape["tile"], mesh.shape["wave"]),
        mesh=mesh, in_specs=placed, out_specs=P("tile", "wave", None), check_vma=False,
    )
```

time: 235 us -> 97.5 us (0.41)
  the two profiles are of different devices: /device:TPU:25 before, /device:TPU:1 now
where the time goes in v1:
time: 97.5 us; the launch traced here: 97.3 us
  Pallas kernels  77.5 us (79%)
  matrix products  14.1 us (14%)
  local copies, waits for them, and re-layouts  5.56 us (6%)
    pallas_call x1, Pallas kernels, shards(): pl.pallas_call(functools.partial(kernel, half, n_tile, n_wave), out_shape...  77.5 us
    dot_general x1, matrix products, shards(): jnp.dot(tau.reshape(rows * cols, waves), profile_basis.T, preferred_eleme...  14.1 us
    unnamed x3, local copies, waits for them, and re-layouts  4.27 us

profile of v1, /device:TPU:1, one launch (start us, length us, event | category | flops | bytes accessed | tf_op | source)
XLA Modules:
  0.0 97.3 jit_solution(9020476754229173852)
XLA Ops:
  0.0 1.3 %pad.4.psf_ref = bf16[32,128]{1,0:T(8,128)(2,1)} pad(bf16[17,17]{1,0:T(8,128)(2,1)} %param.6, bf16[]{:T(256)} %constant.2.clone.1), padding=0_15x0_111 | pad | bytes 8772 | tf_op jit(solution)/shard_map/jit(_pad)/pad | solution.py:241
  1.3 4.3 %copy.5 = bf16[512,16,128]{0,2,1:T(8,128)(2,1)} copy(bf16[512,16,128]{2,1,0:T(8,128)(2,1)} %param.7) | data formatting | bytes 4194304 | tf_op args[3]
  5.6 0.0 copy-start
  5.6 77.5 %shard_map.46 = bf16[16,128,512]{2,1,0:T(8,128)(2,1)} custom-call(bf16[16,128,4096]{2,1,0:T(8,128)(2,1)} %coef_ref.1, bf16[4096,512]{1,0:T(8,128)(2,1)} %basis_hbm.1, bf16[32,128]{1,0:T(8,128)(2,1)} %pad.4.psf_ref, bf16[16,128,512]{2,1,0:T(8,128)(2,1)} %bitcast.5), custom_call_target="tpu_custom_call" | custom-call | tf_op jit(solution)/shard_map/pallas_call | solution.py:247
  83.1 0.0 copy-done
  83.1 14.1 %convolution_convert_fusion = bf16[2048,4096]{1,0:T(8,128)(2,1)} fusion(bf16[2048,512]{1,0:T(8,128)(2,1)} %bitcast.6, bf16[4096,512]{1,0:T(8,128)(2,1)S(1)} %copy-done), kind=kOutput, calls=%fused_computation | convolution fusion | flops 8598323200 | bytes 23068672 | tf_op jit(solution)/shard_map/dot_general | solution.py:269
Async XLA Ops:
  5.6 77.6 %copy-start = (bf16[4096,512]{1,0:T(8,128)(2,1)S(1)}, bf16[4096,512]{1,0:T(8,128)(2,1)}, u32[]{:S(2)}) copy-start(bf16[4096,512]{1,0:T(8,128)(2,1)} %basis_hbm.1) | copy-start | bytes 12582916

commit v2 on v1

--- a/solution.py
+++ b/solution.py
@@ -63,6 +63,10 @@
         "up": {"tile": tile - 1}, "down": {"tile": tile + 1},
         "left": {"wave": wave - 1}, "right": {"wave": wave + 1},
     }
+    for row in ("up", "down"):
+        for col in ("left", "right"):
+            has[row + col] = jnp.logical_and(has[row], has[col])
+            device[row + col] = {**device[row], **device[col]}
     odd = lax.rem(tile, 2)
     steps = rows // TILE_ROWS
     per_half = steps // 2
@@ -100,11 +104,11 @@
 
         @pl.when(jnp.logical_not(has["left"]))
         def _(field=field):
-            field[half:half + rows, 0:EDGE] = jnp.zeros((rows, EDGE, waves), field.dtype)
+            field[:, 0:EDGE] = jnp.zeros((field.shape[0], EDGE, waves), field.dtype)
 
         @pl.when(jnp.logical_not(has["right"]))
         def _(field=field):
-            field[half:half + rows, EDGE + cols:] = jnp.zeros((rows, EDGE, waves), field.dtype)
+            field[:, EDGE + cols:] = jnp.zeros((field.shape[0], EDGE, waves), field.dtype)
 
     peers = jnp.int32(0)
     for side in has:
@@ -119,10 +123,10 @@
         COL_LEFT: ("left", "right", (half, rows), EDGE, EDGE + cols),
         ROW_UP: ("up", "down", (top, near), EDGE, EDGE),
         ROW_DOWN: ("down", "up", (low, 0), EDGE, EDGE),
-        UP_LEFT: ("up", "down", (top, near), 0, 0),
-        UP_RIGHT: ("up", "down", (top, near), EDGE + cols, EDGE + cols),
-        DOWN_LEFT: ("down", "up", (low, 0), 0, 0),
-        DOWN_RIGHT: ("down", "up", (low, 0), EDGE + cols, EDGE + cols),
+        UP_LEFT: ("upleft", "downright", (top, near), EDGE, EDGE + cols),
+        UP_RIGHT: ("upright", "downleft", (top, near), cols, 0),
+        DOWN_LEFT: ("downleft", "upright", (low, 0), EDGE, EDGE + cols),
+        DOWN_RIGHT: ("downright", "upleft", (low, 0), cols, 0),
     }
 
     def copy(which, chunk, kind):
@@ -155,7 +159,9 @@
             def _(kind=kind):
                 copy(which, chunk, kind).wait_recv()
 
-    corners = (UP_LEFT, UP_RIGHT, DOWN_LEFT, DOWN_RIGHT)
+    ups = (UP_LEFT, UP_RIGHT, ROW_UP)
+    downs = (DOWN_LEFT, DOWN_RIGHT, ROW_DOWN)
+    every = ups + downs + (COL_RIGHT, COL_LEFT)
 
     basis_copy.wait()
     for part in range(2):
@@ -175,23 +181,16 @@
                 )
 
             upper = odd if part == 1 else 1 - odd
-
-            @pl.when(jnp.logical_and(upper == 1, has["up"]))
-            def _(chunk=chunk):
-                copy(0, chunk, ROW_UP).start()
-
-            @pl.when(jnp.logical_and(upper == 0, has["down"]))
-            def _(chunk=chunk):
-                copy(0, chunk, ROW_DOWN).start()
+            for wanted, kinds in ((1, ups), (0, downs)):
+                @pl.when(upper == wanted)
+                def _(chunk=chunk, kinds=kinds):
+                    start(0, chunk, kinds)
 
             if part == 1:
                 start(0, chunk, (COL_RIGHT, COL_LEFT))
 
     stencil_matrix(psf_ref, fwd, half, False)
     stencil_matrix(psf_ref, adj, half, True)
-    for chunk in range(CHUNKS):
-        arrive(0, chunk, (COL_RIGHT, COL_LEFT))
-        start(0, chunk, corners)
     obs_copy.wait()
 
     def window(field, i, lanes):
@@ -200,7 +199,7 @@
 
     for chunk in range(CHUNKS):
         lanes = pl.ds(chunk * width, width)
-        arrive(0, chunk, (ROW_UP, ROW_DOWN) + corners)
+        arrive(0, chunk, every)
 
         @pl.loop(0, cols // PATCH)
         def _(i, lanes=lanes):
@@ -210,13 +209,11 @@
                 blurred.reshape(rows, PATCH, width) - seen
             ).astype(jnp.bfloat16)
 
-        start(1, chunk, (COL_RIGHT, COL_LEFT, ROW_UP, ROW_DOWN))
-        arrive(1, chunk, (COL_RIGHT, COL_LEFT))
-        start(1, chunk, corners)
+        start(1, chunk, every)
 
     for chunk in range(CHUNKS):
         lanes = pl.ds(chunk * width, width)
-        arrive(1, chunk, (ROW_UP, ROW_DOWN) + corners)
+        arrive(1, chunk, every)
 
         @pl.loop(0, cols // PATCH)
         def _(i, lanes=lanes):
@@ -238,7 +235,7 @@
     rows, cols, profiles = coefficients.shape
     waves = profile_basis.shape[1]
     half = point_spread.shape[0] // 2
-    psf = jnp.pad(point_spread, ((0, 32 - point_spread.shape[0]), (0, 128 - point_spread.shape[1])))
+    psf = point_spread
     seen = observed.transpose(1, 2, 0)
     padded = (rows + 2 * half, cols + 2 * EDGE, waves)
     table = (PATCH * PATCH, (PATCH + 2 * half) * (PATCH + 2 * EDGE))

time: 97.5 us -> 85.5 us (0.88)
  the two profiles are of different devices: /device:TPU:1 before, /device:TPU:25 now
where the time goes in v2:
time: 85.5 us; the launch traced here: 85.3 us
  Pallas kernels  66.8 us (78%)
  matrix products  14.1 us (16%)
  local copies, waits for them, and re-layouts  4.27 us (5%)
    pallas_call x1, Pallas kernels, shards(): pl.pallas_call(functools.partial(kernel, half, n_tile, n_wave), out_shape...  66.8 us
    dot_general x1, matrix products, shards(): jnp.dot(tau.reshape(rows * cols, waves), profile_basis.T, preferred_eleme...  14.1 us
    unnamed x3, local copies, waits for them, and re-layouts  4.27 us

profile of v2, /device:TPU:25, one launch (start us, length us, event | category | flops | bytes accessed | tf_op | source)
XLA Modules:
  0.0 85.3 jit_solution(14461315862719908015)
XLA Ops:
  0.0 4.3 %copy.5 = bf16[512,16,128]{0,2,1:T(8,128)(2,1)} copy(bf16[512,16,128]{2,1,0:T(8,128)(2,1)} %param.7) | data formatting | bytes 4194304 | tf_op args[3]
  4.3 0.0 copy-start
  4.3 66.8 %shard_map.46 = bf16[16,128,512]{2,1,0:T(8,128)(2,1)} custom-call(bf16[16,128,4096]{2,1,0:T(8,128)(2,1)} %coef_ref.1, bf16[4096,512]{1,0:T(8,128)(2,1)} %basis_hbm.1, bf16[17,17]{1,0:T(8,128)(2,1)} %psf_ref.1, bf16[16,128,512]{2,1,0:T(8,128)(2,1)} %bitcast.5), custom_call_target="tpu_custom_call" | custom-call | tf_op jit(solution)/shard_map/pallas_call | solution.py:244
  71.1 0.0 copy-done
  71.1 14.1 %convolution_convert_fusion = bf16[2048,4096]{1,0:T(8,128)(2,1)} fusion(bf16[2048,512]{1,0:T(8,128)(2,1)} %bitcast.6, bf16[4096,512]{1,0:T(8,128)(2,1)S(1)} %copy-done), kind=kOutput, calls=%fused_computation | convolution fusion | flops 8598323200 | bytes 23068672 | tf_op jit(solution)/shard_map/dot_general | solution.py:266
Async XLA Ops:
  4.3 66.8 %copy-start = (bf16[4096,512]{1,0:T(8,128)(2,1)S(1)}, bf16[4096,512]{1,0:T(8,128)(2,1)}, u32[]{:S(2)}) copy-start(bf16[4096,512]{1,0:T(8,128)(2,1)} %basis_hbm.1) | copy-start | bytes 12582916
